TPU v7x, 32 devices: a whole 2x2x4 slice. The times are simulated.
32 devices in a mesh: site: 2 (over x), gx: 16 (over z, y, core).
Axes of the slice: x: 2, y: 2, z: 4, core: 2. Of those that a mesh axis runs over, the one named last changes fastest.
Arguments:
- velocity: float32 [3, 256, 32, 128], P(None, ('site', 'gx')), parts along dimension 1, may hold values from -6 to 6
- stress: float32 [6, 256, 32, 128], P(None, ('site', 'gx')), parts along dimension 1, may hold values from -6 to 6
- material: int32 [128, 32, 128], P('gx'), may hold values from 0 to 7
- buoyancy_table: float32 [8], replicated, may hold values from 0.7 to 1.4
- lame_table: float32 [8], replicated, may hold values from 0.1 to 0.3
- shear_table: float32 [8], replicated, may hold values from 0.1 to 0.35
- fault_cells: int32 [64, 128], P('gx'), may hold values from 0 to 32767
- block_count: int32 [16], P('gx'), may hold values from 1 to 4, as said below
- strain_history: bfloat16 [128, 6, 128, 512], P(('site', 'gx')), parts along dimension 0, may hold values from -6 to 6
- slip_weights: bfloat16 [64, 256, 768], P('gx'), may hold values from -0.0390625 to 0.0390625
Outputs:
- velocity_out: float32 [3, 256, 32, 128], P(None, ('site', 'gx')), parts along dimension 1
- stress_out: float32 [6, 256, 32, 128], P(None, ('site', 'gx')), parts along dimension 1
- seismograms: float32 [512, 512], P(('site', 'gx')), parts along dimension 0
There are 2 independent parts, one for each index of `site`. A program takes and returns all parts, laid end to end along the dimension named above; an argument that names none is the same for every part. Nothing has to cross between parts.
Inputs may be any that keep to these rules, and one draw needn't show every extreme that they name: `block_count`: live blocks of a device are its first slots; some device has 4 of them. `fault_cells`: cells are numbered row-major over one device's 8 x 32 x 128 slab.
All inputs are finite; a program needn't handle non-finite values.
Results may differ from a plain program's by a relative error of at most 0.00049.
Values may be sent and summed in bfloat16 or wider, within the bound.
No kernel may reach another device: no remote copies, remote signals or barrier semaphores. Data moves between devices by JAX's collectives and lax.ppermute only.
A program may use at most 128 MiB of HBM per device.

v0:
```python
import functools

import jax
import jax.numpy as jnp
from jax import lax
from jax.experimental import pallas as pl
from jax.experimental.pallas import tpu as pltpu
from jax.sharding import PartitionSpec as P

time_step = 0.4
scale = time_step / 24.0

VX, VY, VZ, SXX, SYY, SZZ, SXY, SXZ, SYZ, MAT = range(10)
LOWER_RAW = (2, 1, 1, 3, 1, 1, 3, 3, 1, 3)
UPPER_RAW = (1, 2, 2, 3, 2, 2, 3, 3, 2, 3)
LOWER_MOVED = ((3, 5), (2, 4), (2, 4))
UPPER_MOVED = ((2, 4), (3, 5), (3, 5))
LOWER_FINE = (VX, VY, VZ, SXX, SXY, SXZ, SYZ)
UPPER_FINE = (VY, VZ, SXX)
RAW, MOVED, FINE = range(3)
EDGE = 5
RIM = 8


def halo_list(raw, moved, fine):
    entries = [(RAW, field, depth) for field in range(10) for depth in range(1, raw[field] + 1)]
    for field, (first, last) in enumerate(moved):
        entries += [(MOVED, field, depth) for depth in range(first, last + 1)]
    return entries + [(FINE, field, 1) for field in fine]


LOWER = halo_list(LOWER_RAW, LOWER_MOVED, LOWER_FINE)
UPPER = halo_list(UPPER_RAW, UPPER_MOVED, UPPER_FINE)
HALO = max(len(LOWER), len(UPPER))

f32 = jnp.float32
bf16 = jnp.bfloat16


def second_core():
    return lax.axis_index("gx") % 2


def fetch_all(sources, targets, sems):
    copies = [
        pltpu.make_async_copy(source, target, sems.at[index])
        for index, (source, target) in enumerate(zip(sources, targets))
    ]
    for copy in copies:
        copy.start()
    return copies


def looked_up(code, tables):
    results = [jnp.zeros(code.shape, f32) for _ in tables]
    for entry in range(tables[0].shape[0]):
        hit = code == entry + 1
        results = [jnp.where(hit, table[entry], result) for table, result in zip(tables, results)]
    return results


def parts_of(behind, here_low, here_high, ahead):
    return here_high - here_low, ahead - behind


def joined(*parts):
    near, far = parts[0]
    for more_near, more_far in parts[1:]:
        near, far = near + more_near, far + more_far
    return 27.0 * near - far


def shifted(values, place, axis, by):
    size = values.shape[axis]
    inside = place < size - by if by > 0 else place >= -by
    return jnp.where(inside, pltpu.roll(values, -by % size, axis), 0.0)


def along(values, place, axis, forward):
    offsets = (-1, 0, 1, 2) if forward else (-2, -1, 0, 1)
    return parts_of(*[values if by == 0 else shifted(values, place, axis, by) for by in offsets])


def stepping(moving, pulling, rows, lanes):
    inner = pl.ds(RIM, rows)
    lane = lax.broadcasted_iota(jnp.int32, (rows, lanes), 1)

    def store(field, place, values):
        if field < 3:
            moving[field, place, inner] = values
        else:
            pulling[field - 3, place, inner] = values

    def read(field, place, at=inner):
        return moving[field, place, at] if field < 3 else pulling[field - 3, place, at]

    def along_x(field, place, forward):
        start = place - 1 if forward else place - 2
        return parts_of(*[read(field, start + step) for step in range(4)])

    def along_y(field, place, forward):
        start = RIM - 1 if forward else RIM - 2
        return parts_of(*[read(field, place, pl.ds(start + step, rows)) for step in range(4)])

    def along_z(field, place, forward):
        return along(read(field, place), lane, 1, forward)

    def pull(field, place):
        if field == VX:
            return joined(along_x(SXX, place, True), along_y(SXY, place, False), along_z(SXZ, place, False))
        if field == VY:
            return joined(along_x(SXY, place, False), along_y(SYY, place, True), along_z(SYZ, place, False))
        return joined(along_x(SXZ, place, False), along_y(SYZ, place, False), along_z(SZZ, place, True))

    return store, read, along_x, along_y, along_z, pull


def pack_kernel(
    velocity_from,
    stress_from,
    material_from,
    buoyancy_from,
    weights_from,
    across,
    within,
    weights,
    moving,
    pulling,
    material,
    buoyancy,
    sems,
    weights_sem,
):
    planes, rows, lanes = material.shape
    slab, inner = pl.ds(EDGE, planes), pl.ds(RIM, rows)
    copies = fetch_all(
        (stress_from, velocity_from, material_from, buoyancy_from),
        (pulling.at[:, slab, inner], moving.at[:, slab, inner], material, buoyancy),
        sems,
    )
    weights_copy = pltpu.make_async_copy(weights_from, weights, weights_sem)
    weights_copy.start()
    blank = jnp.zeros((moving.shape[1], RIM, lanes), f32)
    for ref, fields_along_y in ((moving, (0, 1, 2)), (pulling, (SXY - 3, SYY - 3, SYZ - 3))):
        for field in fields_along_y:
            ref[field, :, 0:RIM] = blank
            ref[field, :, RIM + rows : 2 * RIM + rows] = blank
    store, read, along_x, along_y, along_z, pull = stepping(moving, pulling, rows, lanes)
    odd = second_core()
    for copy in copies:
        copy.wait()

    def moved(field, plane):
        factor = scale * looked_up(material[plane] + 1, (buoyancy,))[0]
        return read(field, EDGE + plane) + factor * pull(field, EDGE + plane)

    def fill(out, entries, plane_of):
        for index, (what, field, depth) in enumerate(entries):
            plane = plane_of(depth)
            if what == MOVED:
                values = moved(field, plane)
            elif field < 9:
                values = read(field, EDGE + plane)
            else:
                values = (material[plane] + 1).astype(f32)
            if what == FINE:
                values = values - values.astype(bf16).astype(f32)
            out[index] = values.astype(bf16)
        for spare in range(len(entries), out.shape[0]):
            out[spare] = jnp.zeros(out.shape[1:], bf16)

    def upper_face(out):
        fill(out, LOWER, lambda depth: planes - depth)

    def lower_face(out):
        fill(out, UPPER, lambda depth: depth - 1)

    @pl.when(odd == 0)
    def _():
        lower_face(across)
        upper_face(within)

    @pl.when(odd != 0)
    def _():
        upper_face(across)
        lower_face(within)

    weights_copy.wait()


def history_kernel(live, slips, history, kept, sent, records, total, record_sems):
    slots = slips.shape[0]
    copies = [
        pltpu.make_async_copy(history.at[slot], records.at[slot], record_sems.at[slot]) for slot in range(slots)
    ]
    copies[0].start()
    for slot in range(1, slots):

        @pl.when(slot < live[0])
        def _(slot=slot):
            copies[slot].start()

    copies[0].wait()
    total[...] = jnp.dot(slips[0], records[0], preferred_element_type=f32)
    for slot in range(1, slots):

        @pl.when(slot < live[0])
        def _(slot=slot):
            copies[slot].wait()
            total[...] += jnp.dot(slips[slot], records[slot], preferred_element_type=f32)

    share = kept.shape[1]
    odd = second_core()
    for pair in range(kept.shape[0]):
        even = total[2 * pair * share : (2 * pair + 1) * share]
        other = total[(2 * pair + 1) * share : (2 * pair + 2) * share]
        kept[pair] = jnp.where(odd == 0, even, other)
        sent[pair] = jnp.where(odd == 0, other, even)


def add_kernel(first, second, out):
    out[...] = first[...] + second[...]


def steps_kernel(
    live,
    cells_from,
    buoyancy_from,
    lame_from,
    shear_from,
    material_from,
    velocity,
    stress,
    weights,
    across,
    within,
    velocity_out,
    stress_out,
    tail,
    moving,
    pulling,
    factors,
    strain_factors,
    strains,
    material,
    slips,
    cells,
    buoyancy_table,
    lame_table,
    shear_table,
    scalar_sems,
    slab_sems,
    out_sems,
):
    planes, rows, lanes = velocity.shape[1:]
    tables = (buoyancy_table, lame_table, shear_table)
    inner = pl.ds(RIM, rows)
    slab = pl.ds(EDGE, planes)
    scalar_copies = fetch_all(
        (buoyancy_from, lame_from, shear_from, material_from, cells_from), (*tables, material, cells), scalar_sems
    )
    slab_copies = fetch_all(
        (stress, velocity, weights), (pulling.at[:, slab, inner], moving.at[:, slab, inner], slips), slab_sems
    )
    odd = second_core()
    store, read, along_x, along_y, along_z, pull = stepping(moving, pulling, rows, lanes)

    blank = jnp.zeros((moving.shape[1], RIM, lanes), f32)
    for ref, fields_along_y in ((moving, (0, 1, 2)), (pulling, (SXY - 3, SYY - 3, SYZ - 3))):
        for field in fields_along_y:
            ref[field, :, 0:RIM] = blank
            ref[field, :, RIM + rows : 2 * RIM + rows] = blank

    for copy in scalar_copies:
        copy.wait()
    for plane in range(planes):
        buoyancy, lame, shear = looked_up(material[plane] + 1, tables)
        factors[0, EDGE + plane] = scale * buoyancy
        factors[1, EDGE + plane] = scale * lame
        factors[2, EDGE + plane] = scale * shear
        strain_factors[0, plane] = lame / (3.0 * lame + 2.0 * shear)
        strain_factors[1, plane] = 1.0 / (2.0 * shear)

    def unpack(halo, upper):
        entries = UPPER if upper else LOWER
        for index, (what, field, depth) in enumerate(entries):
            if what == FINE:
                continue
            place = EDGE + planes + depth - 1 if upper else EDGE - depth
            values = halo[index].astype(f32)
            if what == RAW and (FINE, field, depth) in entries:
                values = values + halo[entries.index((FINE, field, depth))].astype(f32)
            if field < 9:
                store(field, place, values)
            else:
                found = looked_up(values.astype(jnp.int32), tables)
                for kind in range(3):
                    factors[kind, place] = scale * found[kind]

    @pl.when(odd == 0)
    def _():
        unpack(across, False)
        unpack(within, True)

    @pl.when(odd != 0)
    def _():
        unpack(within, False)
        unpack(across, True)

    def move(place, do_x=True, do_yz=True):
        buoyancy = factors[0, place]
        chosen = ([VX] if do_x else []) + ([VY, VZ] if do_yz else [])
        results = [read(field, place) + buoyancy * pull(field, place) for field in chosen]
        for field, values in zip(chosen, results):
            store(field, place, values)

    def strain(place, do_yz=True, keep=None):
        lame, shear = factors[1, place], factors[2, place]
        twice = 2.0 * shear
        exx = joined(along_x(VX, place, False))
        eyy = joined(along_y(VY, place, False))
        ezz = joined(along_z(VZ, place, False))
        common = lame * (exx + eyy + ezz)
        changes = [(SXX, common + twice * exx)]
        changes.append((SXY, shear * joined(along_y(VX, place, True), along_x(VY, place, True))))
        changes.append((SXZ, shear * joined(along_z(VX, place, True), along_x(VZ, place, True))))
        if do_yz:
            changes.append((SYY, common + twice * eyy))
            changes.append((SZZ, common + twice * ezz))
            changes.append((SYZ, shear * joined(along_z(VY, place, True), along_y(VZ, place, True))))
        results = {field: read(field, place) + change for field, change in changes}
        for field, values in results.items():
            store(field, place, values)
        if keep is not None:
            compliance = strain_factors[1, place - EDGE]
            shift = strain_factors[0, place - EDGE] * (results[SXX] + results[SYY] + results[SZZ])
            first = pl.multiple_of((place - EDGE) * (8 * rows), 8 * rows)
            for field in range(3, 9):
                values = results[field] - shift if field < 6 else results[field]
                strains[keep, pl.ds(first + field - 3, rows, stride=8)] = values * compliance

    def over(first, last, body, width=2):
        def group(index, carry):
            for step in range(width):
                body(EDGE + first + index * width + step)
            return carry

        lax.fori_loop(0, (last - first) // width, group, 0)

    for copy in slab_copies[:2]:
        copy.wait()
    top = EDGE + planes
    move(EDGE - 2, do_yz=False)
    move(top + 1, do_x=False)
    over(-1, planes + 1, move)
    for place in range(EDGE - 3, EDGE):
        strain(place, do_yz=place == EDGE - 1)
    over(0, planes, functools.partial(strain, keep=0))
    for place in range(top, top + 3):
        strain(place, do_yz=place < top + 2)
    move(EDGE - 2, do_yz=False)
    move(top + 1, do_x=False)
    over(-1, planes + 1, move)
    out_copies = [
        pltpu.make_async_copy(moving.at[:, slab, inner], velocity_out, out_sems.at[0]),
        pltpu.make_async_copy(pulling.at[:, slab, inner], stress_out, out_sems.at[1]),
    ]
    out_copies[0].start()
    over(0, planes, functools.partial(strain, keep=1))
    out_copies[1].start()

    slab_copies[2].wait()
    points_each = cells.shape[1]
    lane_bits = lanes.bit_length() - 1
    tall = lax.broadcasted_iota(jnp.int32, (8, lanes), 1)

    def add_slot(slot, new):
        found = [jnp.zeros((8, lanes), f32) for _ in range(2)]
        for point in range(points_each):
            cell = cells[slot, point]
            first = pl.multiple_of((cell >> lane_bits) << 3, 8)
            shift = (point - cell) & (lanes - 1)
            hit = tall == point
            for which in range(2):
                turned = pltpu.roll(strains[which, pl.ds(first, 8)], shift, 1)
                found[which] = jnp.where(hit, turned, found[which])
        pair = [jnp.concatenate([values[part : part + 1] for part in range(6)], axis=1) for values in found]
        pair = jnp.concatenate(pair + [jnp.zeros((6, 6 * points_each), f32)], axis=0).astype(bf16)
        return new + lax.dot_general(pair, slips[slot], (((1,), (1,)), ((), ())), preferred_element_type=f32)

    new = lax.fori_loop(0, live[0], add_slot, jnp.zeros((8, slips.shape[1]), f32))
    pieces = slips.shape[1] // lanes
    lines = [new[which : which + 1, piece * lanes : (piece + 1) * lanes] for which in range(2) for piece in range(pieces)]
    lines = jnp.concatenate(lines + [jnp.zeros((8 - 2 * pieces, lanes), f32)], axis=0)
    for device in range(tail.shape[0]):
        tail[device] = lines
    for copy in out_copies:
        copy.wait()


def sum_kernel(partials, out):
    share, samples = out.shape
    total = partials[0]
    for chip in range(1, partials.shape[0]):
        total = total + partials[chip]
    out[...] = jnp.concatenate([total[:, 2:], jnp.zeros((share, 2), f32)], axis=1)


def finish_kernel(older, tails, out):
    share, samples = out.shape
    devices, _, lanes = tails.shape
    new = tails[0]
    for device in range(1, devices):
        new = new + tails[device]
    pieces = share * devices // lanes
    row = lax.broadcasted_iota(jnp.int32, (share, lanes), 0) + lax.axis_index("gx") * share
    column = lax.broadcasted_iota(jnp.int32, (share, lanes), 1)
    sample = lax.broadcasted_iota(jnp.int32, (share, samples), 1)
    total = older[...]
    for which in range(2):
        values = jnp.zeros((share, lanes), f32)
        for piece in range(pieces):
            line = which * pieces + piece
            values = values + jnp.where(row == column + piece * lanes, new[line : line + 1], 0.0)
        values = jnp.sum(values, axis=1, keepdims=True)
        total = jnp.where(sample == samples - 2 + which, values, total)
    out[...] = total


def per_device(
    velocity,
    stress,
    material,
    buoyancy_table,
    lame_table,
    shear_table,
    fault_cells,
    block_count,
    strain_history,
    slip_weights,
):
    count = lax.axis_size("gx")
    planes, rows, lanes = material.shape
    slots, parts, points_each, samples = strain_history.shape
    ruptures = slip_weights.shape[1]
    share = ruptures // count
    whole = pl.BlockSpec(memory_space=pltpu.VMEM)
    scalars = pl.BlockSpec(memory_space=pltpu.SMEM)
    anywhere = pl.BlockSpec(memory_space=pl.ANY)
    params = pltpu.CompilerParams(vmem_limit_bytes=24 * 1024 * 1024)

    def stay(array):
        return pltpu.with_memory_space_constraint(array, pltpu.HBM)

    live = block_count
    velocity, stress, material, slip_weights, cells = [
        stay(array) for array in (velocity, stress, material, slip_weights, fault_cells)
    ]
    tables = [stay(table) for table in (buoyancy_table, lame_table, shear_table)]
    table_scratch = [pltpu.SMEM(table.shape, f32) for table in tables]
    history = stay(strain_history.reshape(slots, parts * points_each, samples))

    def cost(flops, size):
        return pl.CostEstimate(flops=flops, bytes_accessed=size, transcendentals=0)

    halo = pltpu.VMEM((HALO, rows, lanes), bf16)
    extent = planes + 2 * EDGE
    padded = [pltpu.VMEM((fields, extent, rows + 2 * RIM, lanes), f32) for fields in (3, 6)]
    across, within, slips = pl.pallas_call(
        pack_kernel,
        out_shape=(halo, halo, pltpu.VMEM(slip_weights.shape, bf16)),
        in_specs=[anywhere] * 5,
        out_specs=(whole,) * 3,
        scratch_shapes=[
            *padded,
            pltpu.VMEM(material.shape, jnp.int32),
            table_scratch[0],
            pltpu.SemaphoreType.DMA((4,)),
            pltpu.SemaphoreType.DMA,
        ],
        compiler_params=params,
        name="pack_halos",
    )(velocity, stress, material, tables[0], slip_weights)
    chips = [(i, i + 1) for i in range(1, count - 1, 2)]
    cores = [(i, i + 1) for i in range(0, count - 1, 2)]
    cores = cores + [(j, i) for i, j in cores]
    across = lax.ppermute(across, "gx", chips + [(j, i) for i, j in chips])
    within = lax.ppermute(within, "gx", cores)

    half = pltpu.VMEM((count // 2, share, samples), f32)
    kept, sent = pl.pallas_call(
        history_kernel,
        out_shape=(half, half),
        in_specs=[scalars, whole, anywhere],
        out_specs=(whole, whole),
        scratch_shapes=[
            pltpu.VMEM(history.shape, bf16),
            pltpu.VMEM((ruptures, samples), f32),
            pltpu.SemaphoreType.DMA((slots,)),
        ],
        compiler_params=params,
        cost_estimate=cost(2 * slots * ruptures * parts * points_each * samples, 2 * history.size),
        name="history_product",
    )(live, slips, history)
    received = lax.ppermute(sent, "gx", cores)
    chip_sum = pl.pallas_call(
        add_kernel,
        out_shape=jax.ShapeDtypeStruct((count // 2, share, samples), f32),
        in_specs=[whole] * 2,
        out_specs=whole,
        compiler_params=params,
        cost_estimate=cost(10**6, 1024 * 1024),
        name="add_cores",
    )(kept, received)
    same_core = [list(range(core, count, 2)) for core in range(2)]
    partials = lax.all_to_all(chip_sum, "gx", 0, 0, axis_index_groups=same_core, tiled=True)

    velocity_two, stress_two, tail = pl.pallas_call(
        steps_kernel,
        out_shape=(
            jax.ShapeDtypeStruct(velocity.shape, f32),
            jax.ShapeDtypeStruct(stress.shape, f32),
            jax.ShapeDtypeStruct((count, 8, lanes), f32),
        ),
        in_specs=[scalars] + [anywhere] * 8 + [whole] * 2,
        out_specs=(anywhere, anywhere, whole),
        scratch_shapes=[
            *padded,
            pltpu.VMEM((3, extent, rows, lanes), f32),
            pltpu.VMEM((2, planes, rows, lanes), f32),
            pltpu.VMEM((2, planes * rows * 8, lanes), f32),
            pltpu.VMEM(material.shape, jnp.int32),
            pltpu.VMEM(slip_weights.shape, bf16),
            pltpu.SMEM(cells.shape, jnp.int32),
            *table_scratch,
            pltpu.SemaphoreType.DMA((5,)),
            pltpu.SemaphoreType.DMA((3,)),
            pltpu.SemaphoreType.DMA((2,)),
        ],
        compiler_params=params,
        cost_estimate=cost(10**10, 30 * 1024 * 1024),
        name="two_steps",
    )(live, cells, *tables, material, velocity, stress, slip_weights, across, within)
    tails = lax.all_to_all(tail, "gx", 0, 0, tiled=True)

    older = pl.pallas_call(
        sum_kernel,
        out_shape=pltpu.VMEM((share, samples), f32),
        in_specs=[whole],
        out_specs=whole,
        compiler_params=params,
        cost_estimate=cost(10**6, 1024 * 1024),
        name="sum_partials",
    )(partials)
    seismograms = pl.pallas_call(
        finish_kernel,
        out_shape=jax.ShapeDtypeStruct((share, samples), f32),
        in_specs=[whole, whole],
        out_specs=whole,
        compiler_params=params,
        name="join_samples",
    )(older, tails)
    return (velocity_two, stress_two, seismograms)


def solution(mesh):
    in_specs = (
        P(None, ("site", "gx"), None, None),
        P(None, ("site", "gx"), None, None),
        P("gx", None, None),
        P(),
        P(),
        P(),
        P("gx", None),
        P("gx"),
        P(("site", "gx"), None, None, None),
        P("gx", None, None),
    )
    out_specs = (
        P(None, ("site", "gx"), None, None),
        P(None, ("site", "gx"), None, None),
        P(("site", "gx"), None),
    )
    return jax.shard_map(
        per_device, mesh=mesh, in_specs=in_specs, out_specs=out_specs, check_vma=False
    )
```

profile of v0, /device:TPU:0, one launch (start us, length us, event | category | flops | bytes accessed | tf_op | source)
XLA Modules:
  0.0 38.5 jit_solution(8168047415123983890)
XLA Ops:
  0.6 1.9 %pack_halos.1 = (bf16[35,32,128]{2,1,0:T(8,128)(2,1)S(1)}, bf16[35,32,128]{2,1,0:T(8,128)(2,1)S(1)}, bf16[4,256,768]{2,1,0:T(8,128)(2,1)S(1)}) custom-call(f32[3,8,32,128]{3,2,1,0:T(8,128)} %velocity.1, f32[6,8,32,128]{3,2,1,0:T(8,128)} %stress.1, s32[8,32,128]{2,1,0:T(8,128)} %material_from.3, f32[8]{0:T(128)} %buoyancy_from.3, bf16[4,256,768]{2,1,0:T(8,128)(2,1)} %weights.1), custom_call_target="tpu_custom_call" | custom-call | tf_op jit(solution)/shard_map/pack_halos/pallas_call | solution.py:469
  2.5 0.7 %collective-permute-start = (bf16[35,32,128]{2,1,0:T(8,128)(2,1)S(1)}, bf16[35,32,128]{2,1,0:T(8,128)(2,1)S(1)}, u32[]{:S(2)}, u32[]{:S(2)}) collective-permute-start(bf16[35,32,128]{2,1,0:T(8,128)(2,1)S(1)} %get-tuple-element.11), channel_id=1, source_target_pairs={{1,2},{3,4},{5,6},{7,8},{9,10},{11,12},{13,14},{2,1},{4,3},{6,5},{... | collective-permute-start | bytes 860168 | tf_op jit(solution)/shard_map/ppermute | solution.py:487
  3.2 4.4 %collective-permute-start.1 = (bf16[35,32,128]{2,1,0:T(8,128)(2,1)S(1)}, bf16[35,32,128]{2,1,0:T(8,128)(2,1)S(1)}, u32[]{:S(2)}, u32[]{:S(2)}) collective-permute-start(bf16[35,32,128]{2,1,0:T(8,128)(2,1)S(1)} %get-tuple-element.12), channel_id=1, source_target_pairs={{0,1},{2,3},{4,5},{6,7},{8,9},{10,11},{12,13},{14,15},{1,0},{3,2},... | collective-permute-start | bytes 860168 | tf_op jit(solution)/shard_map/ppermute | solution.py:488
  8.2 1.6 %history_product.1 = (f32[8,16,512]{2,1,0:T(8,128)S(1)}, f32[8,16,512]{2,1,0:T(8,128)S(1)}) custom-call(s32[1]{0:T(128)S(6)} %copy.13.live, bf16[4,256,768]{2,1,0:T(8,128)(2,1)S(1)} %get-tuple-element.15.slips, bf16[4,768,512]{2,1,0:T(8,128)(2,1)} %bitcast.1), custom_call_target="tpu_custom_call" | custom-call | flops 805306368 | bytes 3145728 | tf_op jit(solution)/shard_map/history_product/pallas_call | solution.py:491
  9.8 0.1 collective-permute-start.2
  9.9 1.5 %collective-permute-done.2.second = f32[8,16,512]{2,1,0:T(8,128)S(1)} collective-permute-done((f32[8,16,512]{2,1,0:T(8,128)S(1)}, f32[8,16,512]{2,1,0:T(8,128)S(1)}, u32[]{:S(2)}, u32[]{:S(2)}) %collective-permute-start.2) | collective-permute-done | bytes 262176 | tf_op jit(solution)/shard_map/ppermute | solution.py:505
  11.4 0.7 %add_cores.1 = f32[8,16,512]{2,1,0:T(8,128)} custom-call(f32[8,16,512]{2,1,0:T(8,128)S(1)} %get-tuple-element.16.first, f32[8,16,512]{2,1,0:T(8,128)S(1)} %collective-permute-done.2.second), custom_call_target="tpu_custom_call" | custom-call | flops 1000000 | bytes 1048576 | tf_op jit(solution)/shard_map/add_cores/pallas_call | solution.py:506
  12.2 5.3 %all-to-all-start = ((f32[8,16,512]{2,1,0:T(8,128)}), f32[8,16,512]{2,1,0:T(8,128)S(1)}, u32[]{:S(2)}, u32[]{:S(2)}) async-start(f32[8,16,512]{2,1,0:T(8,128)} %add_cores.1), calls=%async_computation | async-start | bytes 524288 | tf_op jit(solution)/shard_map/all_to_all | solution.py:516
  17.5 0.0 collective-permute-done.across
  17.5 0.0 collective-permute-done.1.within
  17.5 6.2 %two_steps.1 = (f32[3,8,32,128]{3,2,1,0:T(8,128)}, f32[6,8,32,128]{3,2,1,0:T(8,128)}, f32[16,8,128]{2,1,0:T(8,128)}) custom-call(s32[1]{0:T(128)S(6)} %copy.13.live, s32[4,128]{1,0:T(4,128)} %cells_from.1, f32[8]{0:T(128)} %buoyancy_from.3, f32[8]{0:T(128)} %lame_from.1, f32[8]{0:T(128)} %shear_from.1, s32[8,32,128]{2,1,0:T(8,128)} %material_from.3, ...), custom_call_target="tpu_custom_call" | custom-call | flops 10000000000 | bytes 31457280 | tf_op jit(solution)/shard_map/two_steps/pallas_call | solution.py:518
  23.7 3.0 %all-to-all-done.partials = f32[8,16,512]{2,1,0:T(8,128)S(1)} async-done(((f32[8,16,512]{2,1,0:T(8,128)}), f32[8,16,512]{2,1,0:T(8,128)S(1)}, u32[]{:S(2)}, u32[]{:S(2)}) %all-to-all-start) | async-done | bytes 262176 | tf_op jit(solution)/shard_map/all_to_all | solution.py:516
  26.7 4.2 %all-to-all-start.1 = ((f32[16,8,128]{2,1,0:T(8,128)}), f32[16,8,128]{2,1,0:T(8,128)S(1)}, u32[]{:S(2)}, u32[]{:S(2)}) async-start(f32[16,8,128]{2,1,0:T(8,128)} %get-tuple-element.18), calls=%async_computation.1 | async-start | bytes 131072 | tf_op jit(solution)/shard_map/all_to_all | solution.py:544
  30.9 0.1 sum_partials.1.older
  31.0 6.8 %all-to-all-done.1.tails = f32[16,8,128]{2,1,0:T(8,128)S(1)} async-done(((f32[16,8,128]{2,1,0:T(8,128)}), f32[16,8,128]{2,1,0:T(8,128)S(1)}, u32[]{:S(2)}, u32[]{:S(2)}) %all-to-all-start.1) | async-done | bytes 65568 | tf_op jit(solution)/shard_map/all_to_all | solution.py:544
  37.8 0.7 %join_samples.1 = f32[16,512]{1,0:T(8,128)} custom-call(f32[16,512]{1,0:T(8,128)S(1)} %sum_partials.1.older, f32[16,8,128]{2,1,0:T(8,128)S(1)} %all-to-all-done.1.tails), custom_call_target="tpu_custom_call" | custom-call | tf_op jit(solution)/shard_map/join_samples/pallas_call | solution.py:555
Async XLA Ops:
  2.5 15.0 %collective-permute-start = (bf16[35,32,128]{2,1,0:T(8,128)(2,1)S(1)}, bf16[35,32,128]{2,1,0:T(8,128)(2,1)S(1)}, u32[]{:S(2)}, u32[]{:S(2)}) collective-permute-start(bf16[35,32,128]{2,1,0:T(8,128)(2,1)S(1)} %get-tuple-element.11), channel_id=1, source_target_pairs={{1,2},{3,4},{5,6},{7,8},{9,10},{11,12},{13,14},{2,1},{4,3},{6,5},{... | collective-permute-start | bytes 860168 | tf_op jit(solution)/shard_map/ppermute | solution.py:487
  3.2 14.3 %collective-permute-start.1 = (bf16[35,32,128]{2,1,0:T(8,128)(2,1)S(1)}, bf16[35,32,128]{2,1,0:T(8,128)(2,1)S(1)}, u32[]{:S(2)}, u32[]{:S(2)}) collective-permute-start(bf16[35,32,128]{2,1,0:T(8,128)(2,1)S(1)} %get-tuple-element.12), channel_id=1, source_target_pairs={{0,1},{2,3},{4,5},{6,7},{8,9},{10,11},{12,13},{14,15},{1,0},{3,2},... | collective-permute-start | bytes 860168 | tf_op jit(solution)/shard_map/ppermute | solution.py:488
  9.8 1.6 %collective-permute-start.2 = (f32[8,16,512]{2,1,0:T(8,128)S(1)}, f32[8,16,512]{2,1,0:T(8,128)S(1)}, u32[]{:S(2)}, u32[]{:S(2)}) collective-permute-start(f32[8,16,512]{2,1,0:T(8,128)S(1)} %get-tuple-element.17), channel_id=1, source_target_pairs={{0,1},{2,3},{4,5},{6,7},{8,9},{10,11},{12,13},{14,15},{1,0},{3,2},... | collective-permute-start | bytes 786440 | tf_op jit(solution)/shard_map/ppermute | solution.py:505
  12.2 14.5 %all-to-all-start = ((f32[8,16,512]{2,1,0:T(8,128)}), f32[8,16,512]{2,1,0:T(8,128)S(1)}, u32[]{:S(2)}, u32[]{:S(2)}) async-start(f32[8,16,512]{2,1,0:T(8,128)} %add_cores.1), calls=%async_computation | async-start | bytes 524288 | tf_op jit(solution)/shard_map/all_to_all | solution.py:516
  26.7 11.1 %all-to-all-start.1 = ((f32[16,8,128]{2,1,0:T(8,128)}), f32[16,8,128]{2,1,0:T(8,128)S(1)}, u32[]{:S(2)}, u32[]{:S(2)}) async-start(f32[16,8,128]{2,1,0:T(8,128)} %get-tuple-element.18), calls=%async_computation.1 | async-start | bytes 131072 | tf_op jit(solution)/shard_map/all_to_all | solution.py:544
where the time goes:
time: 39 us; the launch traced here: 38.5 us
  starting transfers between devices  14.7 us (38%)
  waiting for transfers between devices  11.4 us (29%)
  Pallas kernels  11.2 us (29%)
  between operations  1.34 us (3%)
    all_to_all x1, waiting for transfers between devices, per_device(): tails = lax.all_to_all(tail, 'gx', 0, 0, tiled=True)  6.81 us
    pallas_call x1, Pallas kernels, per_device(): pl.pallas_call(steps_kernel, out_shape=(jax.ShapeDtypeStruct(velocity.sha...  6.17 us
    all_to_all x1, starting transfers between devices, per_device(): lax.all_to_all(chip_sum, 'gx', 0, 0, axis_index_groups=same_core, tiled=T...  5.32 us
    ppermute x1, starting transfers between devices, per_device(): within = lax.ppermute(within, 'gx', cores)  4.38 us
    all_to_all x1, starting transfers between devices, per_device(): tails = lax.all_to_all(tail, 'gx', 0, 0, tiled=True)  4.2 us
    all_to_all x1, waiting for transfers between devices, per_device(): lax.all_to_all(chip_sum, 'gx', 0, 0, axis_index_groups=same_core, tiled=T...  3.03 us
    pallas_call x1, Pallas kernels, per_device(): pl.pallas_call(pack_kernel, out_shape=(halo, halo, pltpu.VMEM(slip_weight...  1.86 us
    pallas_call x1, Pallas kernels, per_device(): pl.pallas_call(history_kernel, out_shape=(half, half), in_specs=[scalars,...  1.6 us
  transfers between devices with their start and end apart: 5, of which 3 were waited for; matrix products, arithmetic and copies ran while one was open for 0% of the time, Pallas kernels for 22%

commit v1 on v0

--- a/solution.py
+++ b/solution.py
@@ -188,7 +188,7 @@
     weights_copy.wait()
 
 
-def history_kernel(live, slips, history, kept, sent, records, total, record_sems):
+def history_kernel(live, slips, history, partial, records, total, record_sems):
     slots = slips.shape[0]
     copies = [
         pltpu.make_async_copy(history.at[slot], records.at[slot], record_sems.at[slot]) for slot in range(slots)
@@ -209,17 +209,13 @@
             copies[slot].wait()
             total[...] += jnp.dot(slips[slot], records[slot], preferred_element_type=f32)
 
-    share = kept.shape[1]
-    odd = second_core()
-    for pair in range(kept.shape[0]):
-        even = total[2 * pair * share : (2 * pair + 1) * share]
-        other = total[(2 * pair + 1) * share : (2 * pair + 2) * share]
-        kept[pair] = jnp.where(odd == 0, even, other)
-        sent[pair] = jnp.where(odd == 0, other, even)
-
-
-def add_kernel(first, second, out):
-    out[...] = first[...] + second[...]
+    values = total[...]
+    sample = lax.broadcasted_iota(jnp.int32, values.shape, 1)
+    largest = jnp.max(jnp.where(sample < 2, 0.0, jnp.abs(values)), axis=1, keepdims=True)
+    largest = jnp.maximum(largest, 1e-30)
+    exponent = jnp.ceil(jnp.log2(largest)) - 14.0
+    steps = jnp.clip(jnp.round(values * jnp.exp2(-exponent)), -32767.0, 32767.0)
+    partial[...] = jnp.where(sample == 0, exponent, steps).astype(jnp.int32).astype(jnp.int16)
 
 
 def steps_kernel(
@@ -398,11 +394,13 @@
         copy.wait()
 
 
-def sum_kernel(partials, out):
+def sum_kernel(partials, out, values):
     share, samples = out.shape
-    total = partials[0]
-    for chip in range(1, partials.shape[0]):
-        total = total + partials[chip]
+    steps = partials[...].astype(jnp.int32).astype(f32)
+    values[...] = steps * jnp.exp2(steps[:, 0:1])
+    total = values[0:share]
+    for device in range(1, partials.shape[0] // share):
+        total = total + values[device * share : (device + 1) * share]
     out[...] = jnp.concatenate([total[:, 2:], jnp.zeros((share, 2), f32)], axis=1)
 
 
@@ -487,12 +485,11 @@
     across = lax.ppermute(across, "gx", chips + [(j, i) for i, j in chips])
     within = lax.ppermute(within, "gx", cores)
 
-    half = pltpu.VMEM((count // 2, share, samples), f32)
-    kept, sent = pl.pallas_call(
+    partial = pl.pallas_call(
         history_kernel,
-        out_shape=(half, half),
+        out_shape=jax.ShapeDtypeStruct((ruptures, samples), jnp.int16),
         in_specs=[scalars, whole, anywhere],
-        out_specs=(whole, whole),
+        out_specs=whole,
         scratch_shapes=[
             pltpu.VMEM(history.shape, bf16),
             pltpu.VMEM((ruptures, samples), f32),
@@ -502,18 +499,7 @@
         cost_estimate=cost(2 * slots * ruptures * parts * points_each * samples, 2 * history.size),
         name="history_product",
     )(live, slips, history)
-    received = lax.ppermute(sent, "gx", cores)
-    chip_sum = pl.pallas_call(
-        add_kernel,
-        out_shape=jax.ShapeDtypeStruct((count // 2, share, samples), f32),
-        in_specs=[whole] * 2,
-        out_specs=whole,
-        compiler_params=params,
-        cost_estimate=cost(10**6, 1024 * 1024),
-        name="add_cores",
-    )(kept, received)
-    same_core = [list(range(core, count, 2)) for core in range(2)]
-    partials = lax.all_to_all(chip_sum, "gx", 0, 0, axis_index_groups=same_core, tiled=True)
+    partials = lax.all_to_all(partial, "gx", 0, 0, tiled=True)
 
     velocity_two, stress_two, tail = pl.pallas_call(
         steps_kernel,
@@ -548,6 +534,7 @@
         out_shape=pltpu.VMEM((share, samples), f32),
         in_specs=[whole],
         out_specs=whole,
+        scratch_shapes=[pltpu.VMEM((ruptures, samples), f32)],
         compiler_params=params,
         cost_estimate=cost(10**6, 1024 * 1024),
         name="sum_partials",

time: 39 us -> 37.5 us (0.962)
  starting transfers between devices: 14.7 us -> 13.5 us
  waiting for transfers between devices: 11.4 us -> 10.5 us
    ppermute x1 -> x0, waiting for transfers between devices: 1.52 us -> none  [per_device(): received = lax.ppermute(sent, 'gx', cores)]
    all_to_all x1, waiting for transfers between devices: 3.03 us -> 3.85 us  [per_device(): partials = lax.all_to_all(partial, 'gx', 0, 0, tiled=True)]
    all_to_all x1, starting transfers between devices: 4.2 us -> 3.49 us  [per_device(): tails = lax.all_to_all(tail, 'gx', 0, 0, tiled=True)]
    pallas_call x2 -> x1, Pallas kernels: 2.32 us -> 2.45 us  [per_device(): pl.pallas_call(history_kernel, out_shape=jax.ShapeDtypeStruct((ruptures,...]
  transfers between devices with their start and end apart: 5 -> 4, of which waited for: 3 -> 2; matrix products, arithmetic and copies ran while one was open for 0% -> 0% of each run, Pallas kernels for 22% -> 24%
where the time goes in v1:
time: 37.5 us; the launch traced here: 36.8 us
  starting transfers between devices  13.5 us (36%)
  Pallas kernels  11.4 us (30%)
  waiting for transfers between devices  10.5 us (28%)
  between operations  1.35 us (4%)
    all_to_all x1, waiting for transfers between devices, per_device(): tails = lax.all_to_all(tail, 'gx', 0, 0, tiled=True)  6.68 us
    pallas_call x1, Pallas kernels, per_device(): pl.pallas_call(steps_kernel, out_shape=(jax.ShapeDtypeStruct(velocity.sha...  6.17 us
    all_to_all x1, starting transfers between devices, per_device(): partials = lax.all_to_all(partial, 'gx', 0, 0, tiled=True)  4.99 us
    ppermute x1, starting transfers between devices, per_device(): within = lax.ppermute(within, 'gx', cores)  4.38 us
    all_to_all x1, waiting for transfers between devices, per_device(): partials = lax.all_to_all(partial, 'gx', 0, 0, tiled=True)  3.85 us
    all_to_all x1, starting transfers between devices, per_device(): tails = lax.all_to_all(tail, 'gx', 0, 0, tiled=True)  3.49 us
    pallas_call x1, Pallas kernels, per_device(): pl.pallas_call(history_kernel, out_shape=jax.ShapeDtypeStruct((ruptures,...  2.45 us
    pallas_call x1, Pallas kernels, per_device(): pl.pallas_call(pack_kernel, out_shape=(halo, halo, pltpu.VMEM(slip_weight...  1.86 us
  transfers between devices with their start and end apart: 4, of which 2 were waited for; matrix products, arithmetic and copies ran while one was open for 0% of the time, Pallas kernels for 24%

profile of v1, /device:TPU:0, one launch (start us, length us, event | category | flops | bytes accessed | tf_op | source)
XLA Modules:
  0.0 36.8 jit_solution(16855032034431892657)
XLA Ops:
  0.6 1.9 %pack_halos.1 = (bf16[35,32,128]{2,1,0:T(8,128)(2,1)S(1)}, bf16[35,32,128]{2,1,0:T(8,128)(2,1)S(1)}, bf16[4,256,768]{2,1,0:T(8,128)(2,1)S(1)}) custom-call(f32[3,8,32,128]{3,2,1,0:T(8,128)} %velocity.1, f32[6,8,32,128]{3,2,1,0:T(8,128)} %stress.1, s32[8,32,128]{2,1,0:T(8,128)} %material_from.3, f32[8]{0:T(128)} %buoyancy_from.3, bf16[4,256,768]{2,1,0:T(8,128)(2,1)} %weights.1), custom_call_target="tpu_custom_call" | custom-call | tf_op jit(solution)/shard_map/pack_halos/pallas_call | solution.py:467
  2.5 0.7 %collective-permute-start = (bf16[35,32,128]{2,1,0:T(8,128)(2,1)S(1)}, bf16[35,32,128]{2,1,0:T(8,128)(2,1)S(1)}, u32[]{:S(2)}, u32[]{:S(2)}) collective-permute-start(bf16[35,32,128]{2,1,0:T(8,128)(2,1)S(1)} %get-tuple-element.9), channel_id=1, source_target_pairs={{1,2},{3,4},{5,6},{7,8},{9,10},{11,12},{13,14},{2,1},{4,3},{6,5},{... | collective-permute-start | bytes 860168 | tf_op jit(solution)/shard_map/ppermute | solution.py:485
  3.2 4.4 %collective-permute-start.1 = (bf16[35,32,128]{2,1,0:T(8,128)(2,1)S(1)}, bf16[35,32,128]{2,1,0:T(8,128)(2,1)S(1)}, u32[]{:S(2)}, u32[]{:S(2)}) collective-permute-start(bf16[35,32,128]{2,1,0:T(8,128)(2,1)S(1)} %get-tuple-element.10), channel_id=1, source_target_pairs={{0,1},{2,3},{4,5},{6,7},{8,9},{10,11},{12,13},{14,15},{1,0},{3,2},... | collective-permute-start | bytes 860168 | tf_op jit(solution)/shard_map/ppermute | solution.py:486
  8.2 2.4 %history_product.1 = s16[256,512]{1,0:T(8,128)(2,1)} custom-call(s32[1]{0:T(128)S(6)} %copy.13.live, bf16[4,256,768]{2,1,0:T(8,128)(2,1)S(1)} %get-tuple-element.13.slips, bf16[4,768,512]{2,1,0:T(8,128)(2,1)} %bitcast.4), custom_call_target="tpu_custom_call" | custom-call | flops 805306368 | bytes 3145728 | tf_op jit(solution)/shard_map/history_product/pallas_call | solution.py:488
  10.7 5.0 %all-to-all-start = ((s16[16,16,512]{2,1,0:T(8,128)(2,1)}), s16[16,16,512]{2,1,0:T(8,128)(2,1)S(1)}, u32[]{:S(2)}, u32[]{:S(2)}) async-start(s16[16,16,512]{2,1,0:T(8,128)(2,1)} %bitcast.1), calls=%async_computation | async-start | bytes 524288 | tf_op jit(solution)/shard_map/all_to_all | solution.py:502
  15.7 0.0 collective-permute-done.across
  15.7 0.0 collective-permute-done.1.within
  15.7 6.2 %two_steps.1 = (f32[3,8,32,128]{3,2,1,0:T(8,128)}, f32[6,8,32,128]{3,2,1,0:T(8,128)}, f32[16,8,128]{2,1,0:T(8,128)}) custom-call(s32[1]{0:T(128)S(6)} %copy.13.live, s32[4,128]{1,0:T(4,128)} %cells_from.1, f32[8]{0:T(128)} %buoyancy_from.3, f32[8]{0:T(128)} %lame_from.1, f32[8]{0:T(128)} %shear_from.1, s32[8,32,128]{2,1,0:T(8,128)} %material_from.3, ...), custom_call_target="tpu_custom_call" | custom-call | flops 10000000000 | bytes 31457280 | tf_op jit(solution)/shard_map/two_steps/pallas_call | solution.py:504
  21.9 3.8 %all-to-all-done = s16[16,16,512]{2,1,0:T(8,128)(2,1)S(1)} async-done(((s16[16,16,512]{2,1,0:T(8,128)(2,1)}), s16[16,16,512]{2,1,0:T(8,128)(2,1)S(1)}, u32[]{:S(2)}, u32[]{:S(2)}) %all-to-all-start) | async-done | bytes 262176 | tf_op jit(solution)/shard_map/all_to_all | solution.py:502
  25.7 3.5 %all-to-all-start.1 = ((f32[16,8,128]{2,1,0:T(8,128)}), f32[16,8,128]{2,1,0:T(8,128)S(1)}, u32[]{:S(2)}, u32[]{:S(2)}) async-start(f32[16,8,128]{2,1,0:T(8,128)} %get-tuple-element.14), calls=%async_computation.1 | async-start | bytes 131072 | tf_op jit(solution)/shard_map/all_to_all | solution.py:530
  29.2 0.2 sum_partials.1.older
  29.4 6.7 %all-to-all-done.1.tails = f32[16,8,128]{2,1,0:T(8,128)S(1)} async-done(((f32[16,8,128]{2,1,0:T(8,128)}), f32[16,8,128]{2,1,0:T(8,128)S(1)}, u32[]{:S(2)}, u32[]{:S(2)}) %all-to-all-start.1) | async-done | bytes 65568 | tf_op jit(solution)/shard_map/all_to_all | solution.py:530
  36.1 0.7 %join_samples.1 = f32[16,512]{1,0:T(8,128)} custom-call(f32[16,512]{1,0:T(8,128)S(1)} %sum_partials.1.older, f32[16,8,128]{2,1,0:T(8,128)S(1)} %all-to-all-done.1.tails), custom_call_target="tpu_custom_call" | custom-call | tf_op jit(solution)/shard_map/join_samples/pallas_call | solution.py:542
Async XLA Ops:
  2.5 13.2 %collective-permute-start = (bf16[35,32,128]{2,1,0:T(8,128)(2,1)S(1)}, bf16[35,32,128]{2,1,0:T(8,128)(2,1)S(1)}, u32[]{:S(2)}, u32[]{:S(2)}) collective-permute-start(bf16[35,32,128]{2,1,0:T(8,128)(2,1)S(1)} %get-tuple-element.9), channel_id=1, source_target_pairs={{1,2},{3,4},{5,6},{7,8},{9,10},{11,12},{13,14},{2,1},{4,3},{6,5},{... | collective-permute-start | bytes 860168 | tf_op jit(solution)/shard_map/ppermute | solution.py:485
  3.2 12.5 %collective-permute-start.1 = (bf16[35,32,128]{2,1,0:T(8,128)(2,1)S(1)}, bf16[35,32,128]{2,1,0:T(8,128)(2,1)S(1)}, u32[]{:S(2)}, u32[]{:S(2)}) collective-permute-start(bf16[35,32,128]{2,1,0:T(8,128)(2,1)S(1)} %get-tuple-element.10), channel_id=1, source_target_pairs={{0,1},{2,3},{4,5},{6,7},{8,9},{10,11},{12,13},{14,15},{1,0},{3,2},... | collective-permute-start | bytes 860168 | tf_op jit(solution)/shard_map/ppermute | solution.py:486
  10.7 15.0 %all-to-all-start = ((s16[16,16,512]{2,1,0:T(8,128)(2,1)}), s16[16,16,512]{2,1,0:T(8,128)(2,1)S(1)}, u32[]{:S(2)}, u32[]{:S(2)}) async-start(s16[16,16,512]{2,1,0:T(8,128)(2,1)} %bitcast.1), calls=%async_computation | async-start | bytes 524288 | tf_op jit(solution)/shard_map/all_to_all | solution.py:502
  25.7 10.4 %all-to-all-start.1 = ((f32[16,8,128]{2,1,0:T(8,128)}), f32[16,8,128]{2,1,0:T(8,128)S(1)}, u32[]{:S(2)}, u32[]{:S(2)}) async-start(f32[16,8,128]{2,1,0:T(8,128)} %get-tuple-element.14), calls=%async_computation.1 | async-start | bytes 131072 | tf_op jit(solution)/shard_map/all_to_all | solution.py:530

commit v2 on v1

--- a/solution.py
+++ b/solution.py
@@ -188,6 +188,12 @@
     weights_copy.wait()
 
 
+def in_steps(values, counted):
+    largest = jnp.max(jnp.where(counted, jnp.abs(values), 0.0), axis=1, keepdims=True)
+    exponent = jnp.ceil(jnp.log2(jnp.maximum(largest, 1e-30))) - 14.0
+    return exponent, jnp.clip(jnp.round(values * jnp.exp2(-exponent)), -32767.0, 32767.0)
+
+
 def history_kernel(live, slips, history, partial, records, total, record_sems):
     slots = slips.shape[0]
     copies = [
@@ -211,10 +217,7 @@
 
     values = total[...]
     sample = lax.broadcasted_iota(jnp.int32, values.shape, 1)
-    largest = jnp.max(jnp.where(sample < 2, 0.0, jnp.abs(values)), axis=1, keepdims=True)
-    largest = jnp.maximum(largest, 1e-30)
-    exponent = jnp.ceil(jnp.log2(largest)) - 14.0
-    steps = jnp.clip(jnp.round(values * jnp.exp2(-exponent)), -32767.0, 32767.0)
+    exponent, steps = in_steps(values, sample >= 2)
     partial[...] = jnp.where(sample == 0, exponent, steps).astype(jnp.int32).astype(jnp.int16)
 
 
@@ -230,9 +233,10 @@
     weights,
     across,
     within,
+    partial,
     velocity_out,
     stress_out,
-    tail,
+    sums,
     moving,
     pulling,
     factors,
@@ -244,6 +248,7 @@
     buoyancy_table,
     lame_table,
     shear_table,
+    tail,
     scalar_sems,
     slab_sems,
     out_sems,
@@ -258,6 +263,12 @@
     slab_copies = fetch_all(
         (stress, velocity, weights), (pulling.at[:, slab, inner], moving.at[:, slab, inner], slips), slab_sems
     )
+    samples = partial.shape[1]
+    sum_copies = [
+        pltpu.make_async_copy(partial, sums.at[:, pl.ds(0, samples)], out_sems.at[2]),
+        pltpu.make_async_copy(tail, sums.at[:, pl.ds(samples, lanes)], out_sems.at[3]),
+    ]
+    sum_copies[0].start()
     odd = second_core()
     store, read, along_x, along_y, along_z, pull = stepping(moving, pulling, rows, lanes)
 
@@ -381,48 +392,29 @@
                 turned = pltpu.roll(strains[which, pl.ds(first, 8)], shift, 1)
                 found[which] = jnp.where(hit, turned, found[which])
         pair = [jnp.concatenate([values[part : part + 1] for part in range(6)], axis=1) for values in found]
-        pair = jnp.concatenate(pair + [jnp.zeros((6, 6 * points_each), f32)], axis=0).astype(bf16)
-        return new + lax.dot_general(pair, slips[slot], (((1,), (1,)), ((), ())), preferred_element_type=f32)
-
-    new = lax.fori_loop(0, live[0], add_slot, jnp.zeros((8, slips.shape[1]), f32))
-    pieces = slips.shape[1] // lanes
-    lines = [new[which : which + 1, piece * lanes : (piece + 1) * lanes] for which in range(2) for piece in range(pieces)]
-    lines = jnp.concatenate(lines + [jnp.zeros((8 - 2 * pieces, lanes), f32)], axis=0)
-    for device in range(tail.shape[0]):
-        tail[device] = lines
-    for copy in out_copies:
+        pair = jnp.concatenate(pair + [jnp.zeros((lanes - 2, 6 * points_each), f32)], axis=0).astype(bf16)
+        return new + lax.dot_general(slips[slot], pair, (((1,), (1,)), ((), ())), preferred_element_type=f32)
+
+    new = lax.fori_loop(0, live[0], add_slot, jnp.zeros((slips.shape[1], lanes), f32))
+    column = lax.broadcasted_iota(jnp.int32, new.shape, 1)
+    exponent, steps = in_steps(new, column < 2)
+    tail[...] = jnp.where(column == 2, exponent, steps).astype(jnp.int32).astype(jnp.int16)
+    sum_copies[1].start()
+    for copy in out_copies + sum_copies:
         copy.wait()
 
 
-def sum_kernel(partials, out, values):
+def sum_kernel(sums, out, values, news):
     share, samples = out.shape
-    steps = partials[...].astype(jnp.int32).astype(f32)
+    steps = sums[:, 0:samples].astype(jnp.int32).astype(f32)
     values[...] = steps * jnp.exp2(steps[:, 0:1])
-    total = values[0:share]
-    for device in range(1, partials.shape[0] // share):
-        total = total + values[device * share : (device + 1) * share]
-    out[...] = jnp.concatenate([total[:, 2:], jnp.zeros((share, 2), f32)], axis=1)
-
-
-def finish_kernel(older, tails, out):
-    share, samples = out.shape
-    devices, _, lanes = tails.shape
-    new = tails[0]
-    for device in range(1, devices):
-        new = new + tails[device]
-    pieces = share * devices // lanes
-    row = lax.broadcasted_iota(jnp.int32, (share, lanes), 0) + lax.axis_index("gx") * share
-    column = lax.broadcasted_iota(jnp.int32, (share, lanes), 1)
-    sample = lax.broadcasted_iota(jnp.int32, (share, samples), 1)
-    total = older[...]
-    for which in range(2):
-        values = jnp.zeros((share, lanes), f32)
-        for piece in range(pieces):
-            line = which * pieces + piece
-            values = values + jnp.where(row == column + piece * lanes, new[line : line + 1], 0.0)
-        values = jnp.sum(values, axis=1, keepdims=True)
-        total = jnp.where(sample == samples - 2 + which, values, total)
-    out[...] = total
+    steps = sums[:, samples:].astype(jnp.int32).astype(f32)
+    news[...] = steps * jnp.exp2(steps[:, 2:3])
+    total, new = values[0:share], news[0:share]
+    for device in range(1, sums.shape[0] // share):
+        at = slice(device * share, (device + 1) * share)
+        total, new = total + values[at], new + news[at]
+    out[...] = jnp.concatenate([total[:, 2:], new[:, 0:2]], axis=1)
 
 
 def per_device(
@@ -487,7 +479,7 @@
 
     partial = pl.pallas_call(
         history_kernel,
-        out_shape=jax.ShapeDtypeStruct((ruptures, samples), jnp.int16),
+        out_shape=pltpu.VMEM((ruptures, samples), jnp.int16),
         in_specs=[scalars, whole, anywhere],
         out_specs=whole,
         scratch_shapes=[
@@ -499,17 +491,16 @@
         cost_estimate=cost(2 * slots * ruptures * parts * points_each * samples, 2 * history.size),
         name="history_product",
     )(live, slips, history)
-    partials = lax.all_to_all(partial, "gx", 0, 0, tiled=True)
-
-    velocity_two, stress_two, tail = pl.pallas_call(
+
+    velocity_two, stress_two, sums = pl.pallas_call(
         steps_kernel,
         out_shape=(
             jax.ShapeDtypeStruct(velocity.shape, f32),
             jax.ShapeDtypeStruct(stress.shape, f32),
-            jax.ShapeDtypeStruct((count, 8, lanes), f32),
+            jax.ShapeDtypeStruct((ruptures, samples + lanes), jnp.int16),
         ),
-        in_specs=[scalars] + [anywhere] * 8 + [whole] * 2,
-        out_specs=(anywhere, anywhere, whole),
+        in_specs=[scalars] + [anywhere] * 8 + [whole] * 3,
+        out_specs=(anywhere,) * 3,
         scratch_shapes=[
             *padded,
             pltpu.VMEM((3, extent, rows, lanes), f32),
@@ -519,34 +510,25 @@
             pltpu.VMEM(slip_weights.shape, bf16),
             pltpu.SMEM(cells.shape, jnp.int32),
             *table_scratch,
+            pltpu.VMEM((ruptures, lanes), jnp.int16),
             pltpu.SemaphoreType.DMA((5,)),
             pltpu.SemaphoreType.DMA((3,)),
-            pltpu.SemaphoreType.DMA((2,)),
+            pltpu.SemaphoreType.DMA((4,)),
         ],
         compiler_params=params,
         cost_estimate=cost(10**10, 30 * 1024 * 1024),
         name="two_steps",
-    )(live, cells, *tables, material, velocity, stress, slip_weights, across, within)
-    tails = lax.all_to_all(tail, "gx", 0, 0, tiled=True)
-
-    older = pl.pallas_call(
+    )(live, cells, *tables, material, velocity, stress, slip_weights, across, within, partial)
+    sums = lax.all_to_all(sums, "gx", 0, 0, tiled=True)
+    seismograms = pl.pallas_call(
         sum_kernel,
-        out_shape=pltpu.VMEM((share, samples), f32),
+        out_shape=jax.ShapeDtypeStruct((share, samples), f32),
         in_specs=[whole],
         out_specs=whole,
-        scratch_shapes=[pltpu.VMEM((ruptures, samples), f32)],
+        scratch_shapes=[pltpu.VMEM((ruptures, samples), f32), pltpu.VMEM((ruptures, lanes), f32)],
         compiler_params=params,
-        cost_estimate=cost(10**6, 1024 * 1024),
         name="sum_partials",
-    )(partials)
-    seismograms = pl.pallas_call(
-        finish_kernel,
-        out_shape=jax.ShapeDtypeStruct((share, samples), f32),
-        in_specs=[whole, whole],
-        out_specs=whole,
-        compiler_params=params,
-        name="join_samples",
-    )(older, tails)
+    )(sums)
     return (velocity_two, stress_two, seismograms)
 
 

time: 37.5 us -> 38 us (1.013); the launches traced: 36.8 us -> 38.3 us
  blocking collectives: 0 us -> 21.9 us
  waiting for transfers between devices: 10.5 us -> 0.01 us
  starting transfers between devices: 13.5 us -> 5.06 us
  Pallas kernels: 11.4 us -> 10 us
    all_to_all x0 -> x1, blocking collectives: none -> 21.9 us  [per_device(): sums = lax.all_to_all(sums, 'gx', 0, 0, tiled=True)]
    all_to_all x2 -> x0, waiting for transfers between devices: 10.5 us -> none  [the longest x1 6.68 us: per_device(): tails = lax.all_to_all(tail, 'gx', 0, 0, tiled=True)]
    all_to_all x2 -> x0, starting transfers between devices: 8.48 us -> none  [the longest x1 4.99 us: per_device(): partials = lax.all_to_all(partial, 'gx', 0, 0, tiled=True)]
    pallas_call x3 -> x2, Pallas kernels: 3.34 us -> 2.58 us  [the longest x1 1.75 us: per_device(): pl.pallas_call(history_kernel, out_shape=pltpu.VMEM((ruptures, samples),...]
    pallas_call x1, Pallas kernels: 6.17 us -> 5.58 us  [per_device(): pl.pallas_call(steps_kernel, out_shape=(jax.ShapeDtypeStruct(velocity.sha...]
  transfers between devices with their start and end apart: 4 -> 2, of which waited for: 2 -> 0; matrix products, arithmetic and copies ran while one was open for 0% -> 0% of each run, Pallas kernels for 24% -> 5%
where the time goes in v2:
time: 38 us; the launch traced here: 38.3 us
  blocking collectives  21.9 us (58%)
  Pallas kernels  10 us (26%)
  starting transfers between devices  5.06 us (13%)
  between operations  1.33 us (4%)
    all_to_all x1, blocking collectives, per_device(): sums = lax.all_to_all(sums, 'gx', 0, 0, tiled=True)  21.9 us
    pallas_call x1, Pallas kernels, per_device(): pl.pallas_call(steps_kernel, out_shape=(jax.ShapeDtypeStruct(velocity.sha...  5.58 us
    ppermute x1, starting transfers between devices, per_device(): within = lax.ppermute(within, 'gx', cores)  4.38 us
    pallas_call x1, Pallas kernels, per_device(): pl.pallas_call(pack_kernel, out_shape=(halo, halo, pltpu.VMEM(slip_weight...  1.86 us
    pallas_call x1, Pallas kernels, per_device(): pl.pallas_call(history_kernel, out_shape=pltpu.VMEM((ruptures, samples),...  1.75 us
    pallas_call x1, Pallas kernels, per_device(): pl.pallas_call(sum_kernel, out_shape=jax.ShapeDtypeStruct((share, samples...  0.83 us
  transfers between devices with their start and end apart: 2, of which 0 were waited for; matrix products, arithmetic and copies ran while one was open for 0% of the time, Pallas kernels for 5%

profile of v2, /device:TPU:0, one launch (start us, length us, event | category | flops | bytes accessed | tf_op | source)
XLA Modules:
  0.0 38.3 jit_solution(16199126769577288136)
XLA Ops:
  0.6 1.9 %pack_halos.1 = (bf16[35,32,128]{2,1,0:T(8,128)(2,1)S(1)}, bf16[35,32,128]{2,1,0:T(8,128)(2,1)S(1)}, bf16[4,256,768]{2,1,0:T(8,128)(2,1)S(1)}) custom-call(f32[3,8,32,128]{3,2,1,0:T(8,128)} %velocity.1, f32[6,8,32,128]{3,2,1,0:T(8,128)} %stress.1, s32[8,32,128]{2,1,0:T(8,128)} %material_from.3, f32[8]{0:T(128)} %buoyancy_from.3, bf16[4,256,768]{2,1,0:T(8,128)(2,1)} %weights.1), custom_call_target="tpu_custom_call" | custom-call | tf_op jit(solution)/shard_map/pack_halos/pallas_call | solution.py:459
  2.5 0.7 %collective-permute-start = (bf16[35,32,128]{2,1,0:T(8,128)(2,1)S(1)}, bf16[35,32,128]{2,1,0:T(8,128)(2,1)S(1)}, u32[]{:S(2)}, u32[]{:S(2)}) collective-permute-start(bf16[35,32,128]{2,1,0:T(8,128)(2,1)S(1)} %get-tuple-element.9), channel_id=1, source_target_pairs={{1,2},{3,4},{5,6},{7,8},{9,10},{11,12},{13,14},{2,1},{4,3},{6,5},{... | collective-permute-start | bytes 860168 | tf_op jit(solution)/shard_map/ppermute | solution.py:477
  3.2 4.4 %collective-permute-start.1 = (bf16[35,32,128]{2,1,0:T(8,128)(2,1)S(1)}, bf16[35,32,128]{2,1,0:T(8,128)(2,1)S(1)}, u32[]{:S(2)}, u32[]{:S(2)}) collective-permute-start(bf16[35,32,128]{2,1,0:T(8,128)(2,1)S(1)} %get-tuple-element.10), channel_id=1, source_target_pairs={{0,1},{2,3},{4,5},{6,7},{8,9},{10,11},{12,13},{14,15},{1,0},{3,2},... | collective-permute-start | bytes 860168 | tf_op jit(solution)/shard_map/ppermute | solution.py:478
  8.2 1.8 %history_product.1.partial = s16[256,512]{1,0:T(8,128)(2,1)S(1)} custom-call(s32[1]{0:T(128)S(6)} %copy.13.live, bf16[4,256,768]{2,1,0:T(8,128)(2,1)S(1)} %get-tuple-element.11.slips, bf16[4,768,512]{2,1,0:T(8,128)(2,1)} %bitcast.5), custom_call_target="tpu_custom_call" | custom-call | flops 805306368 | bytes 3145728 | tf_op jit(solution)/shard_map/history_product/pallas_call | solution.py:480
  10.0 0.0 collective-permute-done.across
  10.0 0.0 collective-permute-done.1.within
  10.0 5.6 %two_steps.1 = (f32[3,8,32,128]{3,2,1,0:T(8,128)}, f32[6,8,32,128]{3,2,1,0:T(8,128)}, s16[256,640]{1,0:T(8,128)(2,1)S(1)}) custom-call(s32[1]{0:T(128)S(6)} %copy.13.live, s32[4,128]{1,0:T(4,128)} %cells_from.1, f32[8]{0:T(128)} %buoyancy_from.3, f32[8]{0:T(128)} %lame_from.1, f32[8]{0:T(128)} %shear_from.1, s32[8,32,128]{2,1,0:T(8,128)} %material_from.3, ...), custom_call_target="tpu_custom_call" | custom-call | flops 10000000000 | bytes 31457280 | tf_op jit(solution)/shard_map/two_steps/pallas_call | solution.py:495
  15.6 21.9 %all_to_all.11 = s16[16,16,640]{2,1,0:T(8,128)(2,1)S(1)} all-to-all(s16[16,16,640]{2,1,0:T(8,128)(2,1)S(1)} %bitcast.4), channel_id=1, replica_groups=mesh['site'=2,'gx'=16] {'gx'}, dimensions={0} | all-to-all | bytes 655360 | tf_op jit(solution)/shard_map/all_to_all | solution.py:522
  37.5 0.8 %sum_partials.1 = f32[16,512]{1,0:T(8,128)} custom-call(s16[256,640]{1,0:T(8,128)(2,1)S(1)} %bitcast.3), custom_call_target="tpu_custom_call" | custom-call | tf_op jit(solution)/shard_map/sum_partials/pallas_call | solution.py:523
Async XLA Ops:
  2.5 7.5 %collective-permute-start = (bf16[35,32,128]{2,1,0:T(8,128)(2,1)S(1)}, bf16[35,32,128]{2,1,0:T(8,128)(2,1)S(1)}, u32[]{:S(2)}, u32[]{:S(2)}) collective-permute-start(bf16[35,32,128]{2,1,0:T(8,128)(2,1)S(1)} %get-tuple-element.9), channel_id=1, source_target_pairs={{1,2},{3,4},{5,6},{7,8},{9,10},{11,12},{13,14},{2,1},{4,3},{6,5},{... | collective-permute-start | bytes 860168 | tf_op jit(solution)/shard_map/ppermute | solution.py:477
  3.2 6.8 %collective-permute-start.1 = (bf16[35,32,128]{2,1,0:T(8,128)(2,1)S(1)}, bf16[35,32,128]{2,1,0:T(8,128)(2,1)S(1)}, u32[]{:S(2)}, u32[]{:S(2)}) collective-permute-start(bf16[35,32,128]{2,1,0:T(8,128)(2,1)S(1)} %get-tuple-element.10), channel_id=1, source_target_pairs={{0,1},{2,3},{4,5},{6,7},{8,9},{10,11},{12,13},{14,15},{1,0},{3,2},... | collective-permute-start | bytes 860168 | tf_op jit(solution)/shard_map/ppermute | solution.py:478
